TPU v7x, 32 devices: a whole 2x2x4 slice. The times are simulated.
32 devices in a mesh: groups: 2 (over x), inst: 8 (over z, y), tp: 2 (over core).
Axes of the slice: x: 2, y: 2, z: 4, core: 2. Of those that a mesh axis runs over, the one named last changes fastest.
Arguments:
- queries: bfloat16 [512, 2, 4096], P(('groups', 'inst'), None, 'tp'), parts along dimension 0, may hold values from -21 to 21
- fresh_keys: bfloat16 [512, 2, 512], P(('groups', 'inst'), None, 'tp'), parts along dimension 0, may hold values from -4 to 4
- fresh_values: bfloat16 [512, 2, 512], P(('groups', 'inst'), None, 'tp'), parts along dimension 0, may hold values from -4 to 4
- cache_keys: bfloat16 [512, 128, 512], P(('groups', 'inst'), None, 'tp'), parts along dimension 0, may hold values from -4 to 4
- cache_values: bfloat16 [512, 128, 512], P(('groups', 'inst'), None, 'tp'), parts along dimension 0, may hold values from -12 to 12
- lengths: int32 [512], P(('groups', 'inst')), parts along dimension 0, may hold values from 1 to 126
- move_rows: int32 [16, 4], P(('groups', 'inst')), parts along dimension 0, may hold values from 0 to 31, as said below
- move_targets: int32 [16, 4], P(('groups', 'inst')), parts along dimension 0, may hold values from 0 to 7, as said below
- move_landing: int32 [16, 4], P(('groups', 'inst')), parts along dimension 0, may hold values from 0 to 31, as said below
Outputs:
- first_mixed: bfloat16 [512, 4096], P(('groups', 'inst'), 'tp'), parts along dimension 0
- second_mixed: bfloat16 [512, 4096], P(('groups', 'inst'), 'tp'), parts along dimension 0
- next_keys: bfloat16 [512, 128, 512], P(('groups', 'inst'), None, 'tp'), parts along dimension 0
- next_values: bfloat16 [512, 128, 512], P(('groups', 'inst'), None, 'tp'), parts along dimension 0
There are 2 independent parts, one for each index of `groups`. A program takes and returns all parts, laid end to end along the dimension named above; each array names one. Nothing has to cross between parts.
Inputs may be any that keep to these rules, and one draw needn't show every extreme that they name: `move_rows`: each instance lists 4 different rows of its own. `move_targets`: never the sending instance; for every list position j the j-th entries of all instances name different instances, so every instance receives exactly 4 rows and at most one from each sender. `move_landing`: the rows an instance receives land exactly on the rows that it lists as leaving.
All inputs are finite; a program needn't handle non-finite values.
Results may differ from a plain program's by a relative error of at most 0.0034.
Values may be sent and summed in bfloat16 or wider, within the bound.
A program may use at most 64 MiB of HBM per device.

v0:
```python
import jax
import jax.numpy as jnp
from jax import lax
from jax.sharding import PartitionSpec as P

HQ = 32
KV = 4
HS = 128


masked_score = -1e30


def attend(query_rows, key_rows, value_rows, valid_mask, extra_keys, extra_values):
    row_total = query_rows.shape[0]
    kv_heads = key_rows.shape[-1] // HS
    group_size = HQ // KV
    score_scale = HS ** (-0.5)
    shaped = query_rows.reshape(row_total, kv_heads, group_size, HS)
    cached = (
        jnp.einsum(
            "rkgd,rpkd->rkgp",
            shaped,
            key_rows.reshape(row_total, -1, kv_heads, HS),
            preferred_element_type=jnp.float32,
        )
        * score_scale
    )
    extras = (
        jnp.einsum(
            "rkgd,rekd->rkge",
            shaped,
            extra_keys.reshape(row_total, -1, kv_heads, HS),
            preferred_element_type=jnp.float32,
        )
        * score_scale
    )
    cached = jnp.where(valid_mask[:, None, None, :], cached, masked_score)
    maxima = jnp.maximum(jnp.max(cached, axis=-1), jnp.max(extras, axis=-1))[..., None]
    weights = jnp.where(valid_mask[:, None, None, :], jnp.exp(cached - maxima), 0.0)
    extra_weights = jnp.exp(extras - maxima)
    totals = jnp.sum(weights, axis=-1) + jnp.sum(extra_weights, axis=-1)
    mixed = jnp.einsum(
        "rkgp,rpkd->rkgd",
        weights.astype(jnp.bfloat16),
        value_rows.reshape(row_total, -1, kv_heads, HS),
        preferred_element_type=jnp.float32,
    )
    mixed = mixed + jnp.einsum(
        "rkge,rekd->rkgd",
        extra_weights.astype(jnp.bfloat16),
        extra_values.reshape(row_total, -1, kv_heads, HS),
        preferred_element_type=jnp.float32,
    )
    return (mixed / totals[..., None]).reshape(row_total, -1).astype(jnp.bfloat16)


def on_device(
    queries,
    fresh_keys,
    fresh_values,
    cache_keys,
    cache_values,
    lengths,
    move_rows,
    move_targets,
    move_landing,
):
    row_count = cache_keys.shape[0]
    peer_count = lax.axis_size("inst")
    position = jnp.arange(cache_keys.shape[1], dtype=jnp.int32)
    before = position[None, :] < lengths[:, None]
    first_mixed = attend(
        queries[:, 0], cache_keys, cache_values, before, fresh_keys[:, :1], fresh_values[:, :1]
    )
    all_targets, all_landing = (
        lax.all_gather(move_targets, "inst", axis=0, tiled=True),
        lax.all_gather(move_landing, "inst", axis=0, tiled=True),
    )
    myself = lax.axis_index("inst")
    sources = jnp.arange(peer_count, dtype=jnp.int32)[:, None, None]
    row_ids = jnp.arange(row_count, dtype=jnp.int32)
    incoming = (
        (all_targets == myself)[:, :, None] & (all_landing[:, :, None] == row_ids[None, None, :])
    ).astype(jnp.int32)
    anchor = jnp.sum(incoming * sources, axis=(0, 1))
    landed = jnp.sum(incoming, axis=(0, 1)) > 0
    matches = (move_targets[0][:, None] == jnp.arange(peer_count, dtype=jnp.int32)[None, :]).astype(
        jnp.int32
    )
    send_row = jnp.sum(matches * move_rows[0][:, None], axis=0)
    sending = jnp.sum(matches, axis=0) > 0

    def outgoing(source_rows):
        picked_rows = jnp.take(source_rows, send_row, axis=0)
        wanted = (peer_count,) + (1,) * (source_rows.ndim - 1)
        return jnp.where(sending.reshape(wanted), picked_rows, jnp.zeros_like(picked_rows))

    def settle(received, resident):
        placed = jnp.take(received, anchor, axis=0)
        wanted = (row_count,) + (1,) * (resident.ndim - 1)
        return jnp.where(landed.reshape(wanted), placed, resident)

    def written(key_rows, fresh_rows, row_sizes):
        at_one = (position[None, :] == row_sizes[:, None])[:, :, None]
        at_two = (position[None, :] == row_sizes[:, None] + 1)[:, :, None]
        inside = (position[None, :] < row_sizes[:, None])[:, :, None]
        return jnp.where(
            at_one,
            fresh_rows[:, :1],
            jnp.where(
                at_two, fresh_rows[:, 1:], jnp.where(inside, key_rows, jnp.zeros_like(key_rows))
            ),
        )

    length_marks = lengths.astype(jnp.bfloat16)
    arrived_data = (
        lax.all_to_all(outgoing(cache_keys), "inst", split_axis=0, concat_axis=0, tiled=True),
        lax.all_to_all(outgoing(cache_values), "inst", split_axis=0, concat_axis=0, tiled=True),
        lax.all_to_all(outgoing(fresh_keys), "inst", split_axis=0, concat_axis=0, tiled=True),
        lax.all_to_all(outgoing(fresh_values), "inst", split_axis=0, concat_axis=0, tiled=True),
        lax.all_to_all(outgoing(queries[:, 1]), "inst", split_axis=0, concat_axis=0, tiled=True),
        lax.all_to_all(outgoing(length_marks), "inst", split_axis=0, concat_axis=0, tiled=True),
    )
    post_keys = settle(arrived_data[0], cache_keys)
    post_values = settle(arrived_data[1], cache_values)
    post_fresh_k = settle(arrived_data[2], fresh_keys)
    post_fresh_v = settle(arrived_data[3], fresh_values)
    post_query = settle(arrived_data[4], queries[:, 1])
    post_sizes = settle(arrived_data[5], length_marks).astype(jnp.float32).astype(jnp.int32)
    post_valid = position[None, :] < post_sizes[:, None]
    second_mixed = attend(
        post_query, post_keys, post_values, post_valid, post_fresh_k, post_fresh_v
    )
    next_keys = written(post_keys, post_fresh_k, post_sizes)
    next_values = written(post_values, post_fresh_v, post_sizes)
    return (first_mixed, second_mixed, next_keys, next_values)


def solution(mesh):
    return jax.shard_map(
        on_device,
        mesh=mesh,
        in_specs=(
            P(("groups", "inst"), None, "tp"),
            P(("groups", "inst"), None, "tp"),
            P(("groups", "inst"), None, "tp"),
            P(("groups", "inst"), None, "tp"),
            P(("groups", "inst"), None, "tp"),
            P(("groups", "inst")),
            P(("groups", "inst"), None),
            P(("groups", "inst"), None),
            P(("groups", "inst"), None),
        ),
        out_specs=(
            P(("groups", "inst"), "tp"),
            P(("groups", "inst"), "tp"),
            P(("groups", "inst"), None, "tp"),
            P(("groups", "inst"), None, "tp"),
        ),
        check_vma=False,
    )
```

profile of v0, /device:TPU:0, one launch (start us, length us, event | category | flops | bytes accessed | tf_op | source)
XLA Modules:
  0.0 141.1 jit_solution(6913925453676348797)
XLA Ops:
  0.6 0.8 select_reduce_fusion.1
  1.5 0.7 convert_element_type.46
  2.1 0.6 gather_fusion
  2.8 0.7 copy.76
  3.5 7.3 %all-to-all-start = ((bf16[8,1,1]{2,1,0:T(2,128)(2,1)}), bf16[8,1,1]{2,1,0:T(2,128)(2,1)S(1)}, u32[]{:S(2)}, u32[]{:S(2)}) async-start(bf16[8,1,1]{2,1,0:T(2,128)(2,1)} %copy.76), calls=%async_computation | async-start | bytes 8192 | tf_op jit(solution)/shard_map/all_to_all | solution.py:123
  10.8 0.5 compare_and_fusion
  11.3 0.7 iota_compare_fusion.4
  12.1 1.4 slice_convert_fusion
  13.5 1.3 gather_fusion.10
  14.8 1.9 %gather_fusion.6 = bf16[8,2,256]{2,1,0:T(2,128)(2,1)} fusion(bf16[32,2,256]{2,1,0:T(2,128)(2,1)} %param.18, s32[1024]{0:T(1024)S(1)} %pad_clamp_fusion.1), kind=kCustom, calls=%fused_computation.2.clone | custom fusion | bytes 16416 | tf_op jit(solution)/shard_map/jit(_take)/gather | solution.py:95
  16.7 2.3 %gather_fusion.4 = bf16[8,128,256]{2,1,0:T(8,128)(2,1)S(1)} fusion(bf16[32,128,256]{2,1,0:T(8,128)(2,1)} %param.20, s32[1024]{0:T(1024)S(1)} %pad_clamp_fusion.1), kind=kCustom, calls=%fused_computation.clone | custom fusion | bytes 1048608 | tf_op jit(solution)/shard_map/jit(_take)/gather | solution.py:95
  19.0 2.2 %gather_fusion.8 = bf16[8,128,256]{2,1,0:T(8,128)(2,1)S(1)} fusion(bf16[32,128,256]{2,1,0:T(8,128)(2,1)} %param.21, s32[1024]{0:T(1024)S(1)} %pad_clamp_fusion.1), kind=kCustom, calls=%fused_computation.4.clone | custom fusion | bytes 1048608 | tf_op jit(solution)/shard_map/jit(_take)/gather | solution.py:95
  21.2 1.6 %fusion.73 = (bf16[32,1,2048]{2,1,0:T(2,128)(2,1)S(1)}, bf16[32,2048]{1,0:T(8,128)(2,1)}) fusion(bf16[32,2,2048]{2,1,0:T(2,128)(2,1)S(1)} %copy-done.2), kind=kLoop, calls=%fused_computation.124 | loop fusion | bytes 524288 | tf_op jit(solution)/shard_map/slice | solution.py:122
  22.8 0.1 copy.151
  22.9 0.0 copy-start.10
  22.9 0.0 copy-start.9
  22.9 0.8 gather_fusion.2
  23.7 0.0 copy-start.1
  23.7 1.1 copy.95
  24.8 1.0 fusion.61
  25.8 1.3 fusion.76
  27.1 0.3 fusion.42
  27.5 0.1 fusion.60
  27.6 0.7 broadcast_select_fusion.6
  28.3 1.4 fusion.39
  29.7 6.1 %all-to-all-start.3 = ((bf16[8,2,256]{2,1,0:T(2,128)(2,1)}), bf16[8,2,256]{2,1,0:T(2,128)(2,1)S(1)}, u32[]{:S(2)}, u32[]{:S(2)}) async-start(bf16[8,2,256]{2,1,0:T(2,128)(2,1)} %get-tuple-element.35), calls=%async_computation.3 | async-start | bytes 16384 | tf_op jit(solution)/shard_map/all_to_all | solution.py:120
  35.8 1.2 select_select_fusion.4
  37.0 21.0 %all-gather = s32[8,1,4]{2,1,0:T(1,128)S(1)} all-gather(s32[1,1,4]{2,1,0:T(1,128)S(1)} %bitcast.153), channel_id=1, replica_groups=mesh['groups'=2,'inst'=8,'tp'=2] {'inst'}, dimensions={0}, use_global_device_ids=true | all-gather | bytes 144 | tf_op jit(solution)/shard_map/all_gather | solution.py:77
  58.0 0.1 copy.74
  58.0 3.3 %all-to-all-start.5 = ((bf16[8,2,256]{2,1,0:T(2,128)(2,1)}), bf16[8,2,256]{2,1,0:T(2,128)(2,1)S(1)}, u32[]{:S(2)}, u32[]{:S(2)}) async-start(bf16[8,2,256]{2,1,0:T(2,128)(2,1)} %get-tuple-element.34), calls=%async_computation.5 | async-start | bytes 16384 | tf_op jit(solution)/shard_map/all_to_all | solution.py:121
  61.4 20.8 %all-gather.1 = s32[8,1,4]{2,1,0:T(1,128)S(1)} all-gather(s32[1,1,4]{2,1,0:T(1,128)S(1)} %bitcast.154), channel_id=1, replica_groups=mesh['groups'=2,'inst'=8,'tp'=2] {'inst'}, dimensions={0}, use_global_device_ids=true | all-gather | bytes 144 | tf_op jit(solution)/shard_map/all_gather | solution.py:78
  82.2 0.1 copy.75
  82.3 0.5 broadcast.405
  82.8 0.7 reduce.3
  83.4 0.6 reshape.484
  84.1 3.3 %all-to-all-start.1 = ((bf16[8,2,1024]{2,1,0:T(2,128)(2,1)}), bf16[8,2,1024]{2,1,0:T(2,128)(2,1)S(1)}, u32[]{:S(2)}, u32[]{:S(2)}) async-start(bf16[8,2,1024]{2,1,0:T(2,128)(2,1)} %reshape.484), calls=%async_computation.1 | async-start | bytes 65536 | tf_op jit(solution)/shard_map/all_to_all | solution.py:122
  87.4 0.1 select_reduce_fusion
  87.5 1.6 %copy.150 = bf16[4,8,16,128]{3,1,2,0:T(8,128)(2,1)} copy(bf16[4,8,16,128]{3,2,1,0:T(8,128)(2,1)} %bitcast.141) | data formatting | bytes 262144
  89.1 5.1 %all-to-all-done.1 = bf16[8,2,1024]{2,1,0:T(2,128)(2,1)S(1)} async-done(((bf16[8,2,1024]{2,1,0:T(2,128)(2,1)}), bf16[8,2,1024]{2,1,0:T(2,128)(2,1)S(1)}, u32[]{:S(2)}, u32[]{:S(2)}) %all-to-all-start.1) | async-done | bytes 32800 | tf_op jit(solution)/shard_map/all_to_all | solution.py:122
  94.2 3.5 %all-to-all-start.2 = ((bf16[8,128,256]{2,1,0:T(8,128)(2,1)}), bf16[8,128,256]{2,1,0:T(8,128)(2,1)S(1)}, u32[]{:S(2)}, u32[]{:S(2)}) async-start(bf16[8,128,256]{2,1,0:T(8,128)(2,1)} %get-tuple-element.31), calls=%async_computation.2 | async-start | bytes 1048576 | tf_op jit(solution)/shard_map/all_to_all | solution.py:118
  97.8 0.1 reduce.1
  98.0 0.7 gather_fusion.1
  98.7 0.7 iota_compare_fusion.1
  99.4 12.9 %all-to-all-done.2 = bf16[8,128,256]{2,1,0:T(8,128)(2,1)S(1)} async-done(((bf16[8,128,256]{2,1,0:T(8,128)(2,1)}), bf16[8,128,256]{2,1,0:T(8,128)(2,1)S(1)}, u32[]{:S(2)}, u32[]{:S(2)}) %all-to-all-start.2) | async-done | bytes 524320 | tf_op jit(solution)/shard_map/all_to_all | solution.py:118
  112.3 5.0 %all-to-all-start.4 = ((bf16[8,128,256]{2,1,0:T(8,128)(2,1)}), bf16[8,128,256]{2,1,0:T(8,128)(2,1)S(1)}, u32[]{:S(2)}, u32[]{:S(2)}) async-start(bf16[8,128,256]{2,1,0:T(8,128)(2,1)} %get-tuple-element.30), calls=%async_computation.4 | async-start | bytes 1048576 | tf_op jit(solution)/shard_map/all_to_all | solution.py:119
  117.2 0.6 gather_fusion.7
  117.9 0.6 gather_fusion.11
  118.5 0.2 broadcast_select_fusion
  118.7 0.1 fusion.74
  118.8 0.1 fusion.75
  118.9 0.6 copy.156
  119.6 0.8 gather_fusion.3
  120.4 0.6 copy-done.4
  121.0 0.9 fusion.78
  122.0 2.1 %gather_fusion.5 = bf16[32,128,256]{2,1,0:T(8,128)(2,1)} fusion(bf16[8,128,256]{2,1,0:T(8,128)(2,1)S(1)} %all-to-all-done.2, s32[1024]{0:T(1024)} %copy-done.13), kind=kCustom, calls=%fused_computation.1.clone | custom fusion | bytes 4194432 | tf_op jit(solution)/shard_map/jit(_take)/gather | solution.py:100
  124.1 3.4 %all-to-all-done.4 = bf16[8,128,256]{2,1,0:T(8,128)(2,1)S(1)} async-done(((bf16[8,128,256]{2,1,0:T(8,128)(2,1)}), bf16[8,128,256]{2,1,0:T(8,128)(2,1)S(1)}, u32[]{:S(2)}, u32[]{:S(2)}) %all-to-all-start.4) | async-done | bytes 524320 | tf_op jit(solution)/shard_map/all_to_all | solution.py:119
  127.5 2.1 %gather_fusion.9 = bf16[32,128,256]{2,1,0:T(8,128)(2,1)} fusion(bf16[8,128,256]{2,1,0:T(8,128)(2,1)S(1)} %all-to-all-done.4, s32[1024]{0:T(1024)} %copy-done.13), kind=kCustom, calls=%fused_computation.5.clone | custom fusion | bytes 4194432 | tf_op jit(solution)/shard_map/jit(_take)/gather | solution.py:100
  129.7 7.9 %select_select_fusion.2 = (bf16[32,128,256]{2,1,0:T(8,128)(2,1)}, bf16[32,16,2,8,128]{4,3,2,1,0:T(8,128)(2,1)S(1)}, bf16[32,16,2,8,128]{4,3,2,1,0:T(8,128)(2,1)S(1)}, bf16[32,128,256]{2,1,0:T(8,128)(2,1)}) fusion(pred[32,128]{1,0:T(8,128)(4,1)S(1)} %copy-done.8, pred[32,128]{1,0:T(8,128)(4,1)S(1)} %copy-done.12, pred[32,128]{1,0:T(8,128)(4,1)S(1)} %copy-done.11, ...), kind=kLoop, calls=%fused_computation.26 | loop fusion | flops 10485760 | bytes 16855104 | tf_op jit(solution)/shard_map/jit(_where)/select_n | solution.py:108
  137.6 1.3 fusion.77
  139.0 0.1 fusion.54
  139.1 0.3 fusion.56
  139.4 0.3 fusion.44
  139.7 0.7 fusion.36
  140.4 0.7 copy.149
  (71 shorter events, 0.4 us)
Async XLA Ops:
  0.6 20.6 %copy-start.2 = (bf16[32,2,2048]{2,1,0:T(2,128)(2,1)S(1)}, bf16[32,2,2048]{2,1,0:T(2,128)(2,1)}, u32[]{:S(2)}) copy-start(bf16[32,2,2048]{2,1,0:T(2,128)(2,1)} %param.17) | copy-start | bytes 786436
  1.5 9.9 %copy-start.17 = (s32[1024]{0:T(1024)}, s32[1024]{0:T(1024)S(1)}, u32[]{:S(2)}) copy-start(s32[1024]{0:T(1024)S(1)} %pad_clamp_fusion.3) | copy-start | bytes 12292
  3.5 26.2 %all-to-all-start = ((bf16[8,1,1]{2,1,0:T(2,128)(2,1)}), bf16[8,1,1]{2,1,0:T(2,128)(2,1)S(1)}, u32[]{:S(2)}, u32[]{:S(2)}) async-start(bf16[8,1,1]{2,1,0:T(2,128)(2,1)} %copy.76), calls=%async_computation | async-start | bytes 8192 | tf_op jit(solution)/shard_map/all_to_all | solution.py:123
  16.7 9.1 %copy-start = (bf16[32,128,256]{2,1,0:T(8,128)(2,1)S(1)}, bf16[32,128,256]{2,1,0:T(8,128)(2,1)}, u32[]{:S(2)}) copy-start(bf16[32,128,256]{2,1,0:T(8,128)(2,1)} %param.20) | copy-start | bytes 6291460
  22.8 4.7 %copy-start.14 = (pred[8]{0:T(512)(128)(4,1)S(1)}, pred[8]{0:T(512)(128)(4,1)}, u32[]{:S(2)}) copy-start(pred[8]{0:T(512)(128)(4,1)} %get-tuple-element.47) | copy-start | bytes 28
  22.8 4.7 %copy-start.15 = (pred[8]{0:T(512)(128)(4,1)S(1)}, pred[8]{0:T(512)(128)(4,1)}, u32[]{:S(2)}) copy-start(pred[8]{0:T(512)(128)(4,1)} %get-tuple-element.48) | copy-start | bytes 28
  22.9 4.7 %copy-start.10 = (bf16[8,2,256]{2,1,0:T(2,128)(2,1)S(1)}, bf16[8,2,256]{2,1,0:T(2,128)(2,1)}, u32[]{:S(2)}) copy-start(bf16[8,2,256]{2,1,0:T(2,128)(2,1)} %gather_fusion.6) | copy-start | bytes 24580
  22.9 5.4 %copy-start.9 = (f32[32,1,256]{2,1,0:T(1,128)S(1)}, f32[32,1,256]{2,1,0:T(1,128)}, u32[]{:S(2)}) copy-start(f32[32,1,256]{2,1,0:T(1,128)} %slice_convert_fusion) | copy-start | bytes 98308
  23.7 4.6 %copy-start.1 = (bf16[32,128,256]{2,1,0:T(8,128)(2,1)S(1)}, bf16[32,128,256]{2,1,0:T(8,128)(2,1)}, u32[]{:S(2)}) copy-start(bf16[32,128,256]{2,1,0:T(8,128)(2,1)} %param.21) | copy-start | bytes 6291460
  29.7 7.3 %copy-start.23 = (s32[1,4]{1,0:T(1,128)S(1)}, s32[1,4]{1,0:T(1,128)}, u32[]{:S(2)}) copy-start(s32[1,4]{1,0:T(1,128)} %param.24) | copy-start | bytes 52
  29.7 31.7 %copy-start.24 = (s32[1,4]{1,0:T(1,128)S(1)}, s32[1,4]{1,0:T(1,128)}, u32[]{:S(2)}) copy-start(s32[1,4]{1,0:T(1,128)} %param.25) | copy-start | bytes 52
  29.7 28.4 %all-to-all-start.3 = ((bf16[8,2,256]{2,1,0:T(2,128)(2,1)}), bf16[8,2,256]{2,1,0:T(2,128)(2,1)S(1)}, u32[]{:S(2)}, u32[]{:S(2)}) async-start(bf16[8,2,256]{2,1,0:T(2,128)(2,1)} %get-tuple-element.35), calls=%async_computation.3 | async-start | bytes 16384 | tf_op jit(solution)/shard_map/all_to_all | solution.py:120
  35.8 62.9 %copy-start.22 = (s32[32]{0:T(128)S(1)}, s32[32]{0:T(128)}, u32[]{:S(2)}) copy-start(s32[32]{0:T(128)} %param.22) | copy-start | bytes 388
  37.0 81.5 %copy-start.3 = (bf16[32,2,256]{2,1,0:T(2,128)(2,1)S(1)}, bf16[32,2,256]{2,1,0:T(2,128)(2,1)}, u32[]{:S(2)}) copy-start(bf16[32,2,256]{2,1,0:T(2,128)(2,1)} %param.19) | copy-start | bytes 98308
  37.0 81.6 %copy-start.7 = (bf16[32,2,256]{2,1,0:T(2,128)(2,1)S(1)}, bf16[32,2,256]{2,1,0:T(2,128)(2,1)}, u32[]{:S(2)}) copy-start(bf16[32,2,256]{2,1,0:T(2,128)(2,1)} %param.18) | copy-start | bytes 98308
  58.0 26.0 %all-to-all-start.5 = ((bf16[8,2,256]{2,1,0:T(2,128)(2,1)}), bf16[8,2,256]{2,1,0:T(2,128)(2,1)S(1)}, u32[]{:S(2)}, u32[]{:S(2)}) async-start(bf16[8,2,256]{2,1,0:T(2,128)(2,1)} %get-tuple-element.34), calls=%async_computation.5 | async-start | bytes 16384 | tf_op jit(solution)/shard_map/all_to_all | solution.py:121
  84.1 10.2 %all-to-all-start.1 = ((bf16[8,2,1024]{2,1,0:T(2,128)(2,1)}), bf16[8,2,1024]{2,1,0:T(2,128)(2,1)S(1)}, u32[]{:S(2)}, u32[]{:S(2)}) async-start(bf16[8,2,1024]{2,1,0:T(2,128)(2,1)} %reshape.484), calls=%async_computation.1 | async-start | bytes 65536 | tf_op jit(solution)/shard_map/all_to_all | solution.py:122
  94.2 18.0 %all-to-all-start.2 = ((bf16[8,128,256]{2,1,0:T(8,128)(2,1)}), bf16[8,128,256]{2,1,0:T(8,128)(2,1)S(1)}, u32[]{:S(2)}, u32[]{:S(2)}) async-start(bf16[8,128,256]{2,1,0:T(8,128)(2,1)} %get-tuple-element.31), calls=%async_computation.2 | async-start | bytes 1048576 | tf_op jit(solution)/shard_map/all_to_all | solution.py:118
  97.8 21.1 %copy-start.16 = (s32[1024]{0:T(1024)}, s32[1024]{0:T(1024)S(1)}, u32[]{:S(2)}) copy-start(s32[1024]{0:T(1024)S(1)} %pad_clamp_fusion.2) | copy-start | bytes 12292
  97.8 21.1 %copy-start.18 = (pred[32]{0:T(512)(128)(4,1)}, pred[32]{0:T(512)(128)(4,1)S(1)}, u32[]{:S(2)}) copy-start(pred[32]{0:T(512)(128)(4,1)S(1)} %get-tuple-element.45) | copy-start | bytes 100
  97.8 21.1 %copy-start.20 = (pred[32]{0:T(512)(128)(4,1)}, pred[32]{0:T(512)(128)(4,1)S(1)}, u32[]{:S(2)}) copy-start(pred[32]{0:T(512)(128)(4,1)S(1)} %get-tuple-element.46) | copy-start | bytes 100
  112.3 15.2 %all-to-all-start.4 = ((bf16[8,128,256]{2,1,0:T(8,128)(2,1)}), bf16[8,128,256]{2,1,0:T(8,128)(2,1)S(1)}, u32[]{:S(2)}, u32[]{:S(2)}) async-start(bf16[8,128,256]{2,1,0:T(8,128)(2,1)} %get-tuple-element.30), calls=%async_computation.4 | async-start | bytes 1048576 | tf_op jit(solution)/shard_map/all_to_all | solution.py:119
  117.2 1.7 %copy-start.13 = (s32[1024]{0:T(1024)}, s32[1024]{0:T(1024)S(1)}, u32[]{:S(2)}) copy-start(s32[1024]{0:T(1024)S(1)} %pad_clamp_fusion) | copy-start | bytes 12292
  120.4 0.7 copy-start.4
  124.1 5.5 %copy-start.6 = (bf16[32,1,256]{2,0,1:T(8,128)(2,1)S(1)}, bf16[32,1,256]{2,0,1:T(8,128)(2,1)}, u32[]{:S(2)}) copy-start(bf16[32,1,256]{2,0,1:T(8,128)(2,1)} %copy.156) | copy-start | bytes 49156
  124.1 5.5 %copy-start.8 = (pred[32,128]{1,0:T(8,128)(4,1)S(1)}, pred[32,128]{1,0:T(8,128)(4,1)}, u32[]{:S(2)}) copy-start(pred[32,128]{1,0:T(8,128)(4,1)} %get-tuple-element.37) | copy-start | bytes 12292
  124.1 5.5 %copy-start.11 = (pred[32,128]{1,0:T(8,128)(4,1)S(1)}, pred[32,128]{1,0:T(8,128)(4,1)}, u32[]{:S(2)}) copy-start(pred[32,128]{1,0:T(8,128)(4,1)} %get-tuple-element.36) | copy-start | bytes 12292
  124.1 5.5 %copy-start.12 = (pred[32,128]{1,0:T(8,128)(4,1)S(1)}, pred[32,128]{1,0:T(8,128)(4,1)}, u32[]{:S(2)}) copy-start(pred[32,128]{1,0:T(8,128)(4,1)} %get-tuple-element.49) | copy-start | bytes 12292
  124.1 5.5 %copy-start.19 = (pred[32]{0:T(512)(128)(4,1)S(1)}, pred[32]{0:T(512)(128)(4,1)}, u32[]{:S(2)}) copy-start(pred[32]{0:T(512)(128)(4,1)} %copy-done.18) | copy-start | bytes 100
  124.1 5.5 %copy-start.21 = (pred[32]{0:T(512)(128)(4,1)S(1)}, pred[32]{0:T(512)(128)(4,1)}, u32[]{:S(2)}) copy-start(pred[32]{0:T(512)(128)(4,1)} %copy-done.20) | copy-start | bytes 100
  129.7 7.9 %copy-start.5 = (bf16[4,8,16,128]{3,2,1,0:T(8,128)(2,1)S(1)}, bf16[4,8,16,128]{3,2,1,0:T(8,128)(2,1)}, u32[]{:S(2)}) copy-start(bf16[4,8,16,128]{3,2,1,0:T(8,128)(2,1)} %copy-done.4) | copy-start | bytes 393220
where the time goes:
time: 142 us; the launch traced here: 141 us
  blocking collectives  41.8 us (29%)
  starting transfers between devices  28.6 us (20%)
  local copies, waits for them, and re-layouts  24.8 us (17%)
  waiting for transfers between devices  21.4 us (15%)
  other arithmetic  16.6 us (12%)
  matrix products  6.9 us (5%)
    all_gather x1, blocking collectives, on_device(): lax.all_gather(move_targets, 'inst', axis=0, tiled=True)  21 us
    all_gather x1, blocking collectives, on_device(): lax.all_gather(move_landing, 'inst', axis=0, tiled=True)  20.8 us
    all_to_all x1, waiting for transfers between devices, on_device(): lax.all_to_all(outgoing(cache_keys), 'inst', split_axis=0, concat_axis=0,...  12.9 us
    gather x6, local copies, waits for them, and re-layouts, outgoing(): picked_rows = jnp.take(source_rows, send_row, axis=0)  9.23 us
    select_n x1, other arithmetic, written(): jnp.where(at_one, fresh_rows[:, :1], jnp.where(at_two, fresh_rows[:, 1:],...  7.92 us
    all_to_all x1, starting transfers between devices, on_device(): lax.all_to_all(outgoing(length_marks), 'inst', split_axis=0, concat_axis=...  7.28 us
    gather x6, local copies, waits for them, and re-layouts, settle(): placed = jnp.take(received, anchor, axis=0)  6.98 us
    all_to_all x1, starting transfers between devices, on_device(): lax.all_to_all(outgoing(fresh_keys), 'inst', split_axis=0, concat_axis=0,...  6.13 us
  transfers between devices with their start and end apart: 6, of which 3 were waited for; matrix products, arithmetic and copies ran while one was open for 22% of the time, Pallas kernels for 0%

commit v1 on v0

v1 whole, which is shorter than its diff:
```python
import functools

import jax
import jax.numpy as jnp
from jax import lax
from jax.experimental import pallas as pl
from jax.experimental.pallas import tpu as pltpu
from jax.sharding import PartitionSpec as P

HS = 128
MASKED = -1e30
MESH = pl.DeviceIdType.MESH
UNROLL = 4


def written(cached, fresh, size, place):
    fresh = fresh.astype(jnp.float32)
    cached = cached.astype(jnp.float32)
    out = jnp.where(place < size, cached, 0.0)
    out = jnp.where(place == size, fresh[0:1], out)
    out = jnp.where(place == size + 1, fresh[1:2], out)
    return out.astype(jnp.bfloat16)


def exchange_kernel(
    n,
    lens,
    move_rows,
    move_targets,
    table,
    q,
    fk,
    fv,
    ck_hbm,
    cv_hbm,
    nk,
    nv,
    o_out,
    got,
    got_o,
    got_table,
    ck,
    cv,
    o,
    pack,
    pack_o,
    in_sem,
    out_sem,
    send_sem,
    recv_sem,
):
    me = lax.axis_index("inst")
    rows, ctx, width = ck.shape
    heads = width // HS
    qrows = q.shape[1] // heads
    moves = move_rows.shape[1]

    load_k = pltpu.make_async_copy(ck_hbm, ck, in_sem.at[0])
    load_v = pltpu.make_async_copy(cv_hbm, cv, in_sem.at[1])
    load_k.start()
    load_v.start()

    barrier = pltpu.get_barrier_semaphore()
    for d in range(1, n):
        pl.semaphore_signal(
            barrier, inc=1, device_id={"inst": lax.rem(me + d, n)}, device_id_type=MESH
        )

    place = lax.broadcasted_iota(jnp.int32, (ctx, width), 0)

    def leaving(peer):
        row = jnp.int32(0)
        for j in range(moves):
            row = row + jnp.where(move_targets[0, j] == peer, move_rows[0, j], 0)
        return row

    def remote(src, dst, part, d):
        return pltpu.make_async_remote_copy(
            src_ref=src,
            dst_ref=dst,
            send_sem=send_sem.at[part, d - 1],
            recv_sem=recv_sem.at[part, d - 1],
            device_id={"inst": lax.rem(me + d, n)},
            device_id_type=MESH,
        )

    def send_k(d):
        return remote(pack.at[d - 1, 0], got.at[d - 1, 0], 0, d)

    def send_v(d):
        return remote(pack.at[d - 1, 1], got.at[d - 1, 1], 1, d)

    def send_o(d):
        return remote(pack_o.at[d - 1], got_o.at[d - 1], 2, d)

    def send_table(d):
        return remote(table, got_table.at[d - 1], 3, d)

    load_k.wait()
    pl.semaphore_wait(barrier, n - 1)

    @pl.loop(1, n)
    def _(d):
        row = leaving(lax.rem(me + d, n))
        pack[d - 1, 0] = written(ck[row], fk[row], lens[row], place)
        send_k(d).start()

    load_v.wait()

    @pl.loop(1, n)
    def _(d):
        row = leaving(lax.rem(me + d, n))
        pack[d - 1, 1] = written(cv[row], fv[row], lens[row], place)
        send_v(d).start()

    @pl.loop(1, n)
    def _(d):
        send_table(d).start()

    column = lax.broadcasted_iota(jnp.int32, (qrows, ctx), 1)
    step = jnp.where(lax.broadcasted_iota(jnp.int32, (qrows, ctx), 0) >= qrows // 2, 1, 0)
    offset = column - step
    scale = HS ** (-0.5)

    def save_k(first):
        return pltpu.make_async_copy(
            ck.at[pl.ds(first, UNROLL)], nk.at[pl.ds(first, UNROLL)], out_sem.at[0]
        )

    def save_v(first):
        return pltpu.make_async_copy(
            cv.at[pl.ds(first, UNROLL)], nv.at[pl.ds(first, UNROLL)], out_sem.at[1]
        )

    @pl.loop(0, rows // UNROLL)
    def _(block):
        first = block * UNROLL
        values = []
        scores = []
        for u in range(UNROLL):
            r = first + u
            size = lens[r]
            keys = written(ck[r], fk[r], size, place)
            vals = written(cv[r], fv[r], size, place)
            ck[r] = keys
            cv[r] = vals
            values.append(vals)
            for h in range(heads):
                s = lax.dot_general(
                    q[r, h * qrows : (h + 1) * qrows, :],
                    keys[:, h * HS : (h + 1) * HS],
                    (((1,), (1,)), ((), ())),
                    preferred_element_type=jnp.float32,
                )
                scores.append(jnp.where(offset <= size, s * scale, MASKED))
        save_k(first).start()
        save_v(first).start()
        s = jnp.concatenate(scores, axis=0)
        w = jnp.exp(s - jnp.max(s, axis=1, keepdims=True))
        totals = jnp.sum(w, axis=1, keepdims=True)
        w = w.astype(jnp.bfloat16)
        mixed = []
        for u in range(UNROLL):
            for h in range(heads):
                at = (u * heads + h) * qrows
                mixed.append(
                    lax.dot_general(
                        w[at : at + qrows],
                        values[u][:, h * HS : (h + 1) * HS],
                        (((1,), (0,)), ((), ())),
                        preferred_element_type=jnp.float32,
                    )
                )
        done = (jnp.concatenate(mixed, axis=0) / totals).astype(jnp.bfloat16)
        o[pl.ds(first, UNROLL)] = done.reshape(UNROLL, heads * qrows, HS)

    save_o = pltpu.make_async_copy(o, o_out, in_sem.at[0])
    save_o.start()

    @pl.loop(1, n)
    def _(d):
        row = leaving(lax.rem(me + d, n))
        pack_o[d - 1] = o[row]
        send_o(d).start()

    save_o.wait()
    pltpu.make_async_copy(ck, nk, out_sem.at[0]).wait()
    pltpu.make_async_copy(cv, nv, out_sem.at[1]).wait()

    @pl.loop(1, n)
    def _(d):
        send_table(d).wait()
        send_k(d).wait()
        send_v(d).wait()
        send_o(d).wait()


def place_kernel(
    n, moves, me_ref, table, nk, nv, o, got, got_o, out_k, out_v, out_o, source, sems
):
    rows = nk.shape[0]
    me = me_ref[0]

    @pl.loop(0, rows)
    def _(s):
        source[s] = -1

    @pl.loop(0, n - 1)
    def _(d):
        for j in range(moves):

            @pl.when(table[d, 0, j] == me)
            def _():
                source[table[d, 0, moves + j]] = d

    @pl.loop(0, rows)
    def _(s):
        d = source[s]

        @pl.when(d < 0)
        def _():
            pltpu.make_async_copy(nk.at[s], out_k.at[s], sems.at[0]).start()
            pltpu.make_async_copy(nv.at[s], out_v.at[s], sems.at[1]).start()
            pltpu.make_async_copy(o.at[s], out_o.at[s], sems.at[2]).start()

        @pl.when(d >= 0)
        def _():
            pltpu.make_async_copy(got.at[d, 0], out_k.at[s], sems.at[0]).start()
            pltpu.make_async_copy(got.at[d, 1], out_v.at[s], sems.at[1]).start()
            pltpu.make_async_copy(got_o.at[d], out_o.at[s], sems.at[2]).start()

    pltpu.make_async_copy(nk, out_k, sems.at[0]).wait()
    pltpu.make_async_copy(nv, out_v, sems.at[1]).wait()
    pltpu.make_async_copy(o, out_o, sems.at[2]).wait()


def on_device(
    n,
    queries,
    fresh_keys,
    fresh_values,
    cache_keys,
    cache_values,
    lengths,
    move_rows,
    move_targets,
    move_landing,
):
    rows, ctx, width = cache_keys.shape
    heads = width // HS
    group = queries.shape[2] // HS // heads
    moves = move_rows.shape[1]
    lanes = max(HS, 2 * moves)
    q = (
        queries.reshape(rows, 2, heads, group, HS)
        .transpose(0, 2, 1, 3, 4)
        .reshape(rows, heads * 2 * group, HS)
    )
    table = jnp.pad(
        jnp.concatenate([move_targets, move_landing], axis=1), ((0, 0), (0, lanes - 2 * moves))
    )
    qrows = heads * 2 * group
    bf16 = jnp.bfloat16
    vmem = pl.BlockSpec(memory_space=pltpu.VMEM)
    smem = pl.BlockSpec(memory_space=pltpu.SMEM)
    any_ = pl.BlockSpec(memory_space=pl.ANY)
    shape = jax.ShapeDtypeStruct
    cache = shape((rows, ctx, width), bf16)
    nk, nv, o, got, got_o, got_table = pl.pallas_call(
        functools.partial(exchange_kernel, n),
        out_shape=(
            cache,
            cache,
            shape((rows, qrows, HS), bf16),
            shape((n - 1, 2, ctx, width), bf16),
            shape((n - 1, qrows, HS), bf16),
            shape((n - 1, 1, lanes), jnp.int32),
        ),
        in_specs=[smem, smem, smem, vmem, vmem, vmem, vmem, any_, any_],
        out_specs=(any_,) * 6,
        scratch_shapes=[
            pltpu.VMEM((rows, ctx, width), bf16),
            pltpu.VMEM((rows, ctx, width), bf16),
            pltpu.VMEM((rows, qrows, HS), bf16),
            pltpu.VMEM((n - 1, 2, ctx, width), bf16),
            pltpu.VMEM((n - 1, qrows, HS), bf16),
            pltpu.SemaphoreType.DMA((2,)),
            pltpu.SemaphoreType.DMA((2,)),
            pltpu.SemaphoreType.DMA((4, n - 1)),
            pltpu.SemaphoreType.DMA((4, n - 1)),
        ],
        compiler_params=pltpu.CompilerParams(
            collective_id=0, has_side_effects=True, vmem_limit_bytes=40 * 2**20
        ),
        name="exchange",
    )(lengths, move_rows, move_targets, table, q, fresh_keys, fresh_values, cache_keys, cache_values)
    me = lax.axis_index("inst").astype(jnp.int32).reshape(1)
    next_keys, next_values, settled = pl.pallas_call(
        functools.partial(place_kernel, n, moves),
        out_shape=(cache, cache, shape((rows, qrows, HS), bf16)),
        in_specs=[smem, smem] + [any_] * 5,
        out_specs=(any_,) * 3,
        scratch_shapes=[pltpu.SMEM((rows,), jnp.int32), pltpu.SemaphoreType.DMA((3,))],
        name="place",
    )(me, got_table, nk, nv, o, got, got_o)
    shaped = (rows, heads, 2, group, HS)
    first_mixed = o.reshape(shaped)[:, :, 0].reshape(rows, -1)
    second_mixed = settled.reshape(shaped)[:, :, 1].reshape(rows, -1)
    return first_mixed, second_mixed, next_keys, next_values


def solution(mesh):
    split = P(("groups", "inst"), None, "tp")
    table = P(("groups", "inst"), None)
    return jax.shard_map(
        functools.partial(on_device, mesh.shape["inst"]),
        mesh=mesh,
        in_specs=(split,) * 5 + (P(("groups", "inst")), table, table, table),
        out_specs=(P(("groups", "inst"), "tp"), P(("groups", "inst"), "tp"), split, split),
        check_vma=False,
    )
```

time: 142 us -> 186 us (1.31)
  Pallas kernels: 0 us -> 169 us
  blocking collectives: 41.8 us -> 0 us
  starting transfers between devices: 28.6 us -> 0 us
  waiting for transfers between devices: 21.4 us -> 0 us
  other arithmetic: 16.6 us -> 0.75 us
  local copies, waits for them, and re-layouts: 24.8 us -> 15 us
  matrix products: 6.9 us -> 0 us
    pallas_call x0 -> x2, Pallas kernels: none -> 169 us  [the longest x1 137 us: on_device(): pl.pallas_call(functools.partial(place_kernel, n, moves), out_shape=(cach...]
    all_gather x2 -> x0, blocking collectives: 41.8 us -> none  [the longest x1 21 us: on_device(): lax.all_gather(move_targets, 'inst', axis=0, tiled=True)]
    all_to_all x6 -> x0, starting transfers between devices: 28.6 us -> none  [the longest x1 7.28 us: on_device(): lax.all_to_all(outgoing(length_marks), 'inst', split_axis=0, concat_axis=...]
    all_to_all x6 -> x0, waiting for transfers between devices: 21.4 us -> none  [the longest x1 12.9 us: on_device(): lax.all_to_all(outgoing(cache_keys), 'inst', split_axis=0, concat_axis=0,...]
    gather x12 -> x0, local copies, waits for them, and re-layouts: 16.2 us -> none  [the longest x6 9.23 us: outgoing(): picked_rows = jnp.take(source_rows, send_row, axis=0)]
    select_n x10 -> x0, other arithmetic: 10.7 us -> none  [the longest x1 7.92 us: written(): jnp.where(at_one, fresh_rows[:, :1], jnp.where(at_two, fresh_rows[:, 1:],...]
    dot_general x7 -> x0, matrix products: 6.9 us -> none  [the longest x2 2.63 us: attend(): jnp.einsum('rkgd,rpkd->rkgp', shaped, key_rows.reshape(row_total, -1, kv_...]
    unnamed x63 -> x28, local copies, waits for them, and re-layouts: 5.53 us -> 12.2 us
  transfers between devices with their start and end apart: 6 -> 0, of which waited for: 3 -> 0; matrix products, arithmetic and copies ran while one was open for 22% -> 0% of each run, Pallas kernels for 0% -> 0%
where the time goes in v1:
time: 186 us
  Pallas kernels  169 us (91%)
  local copies, waits for them, and re-layouts  15 us (8%)
    pallas_call x1, Pallas kernels, on_device(): pl.pallas_call(functools.partial(place_kernel, n, moves), out_shape=(cach...  137 us
    pallas_call x1, Pallas kernels, on_device(): pl.pallas_call(functools.partial(exchange_kernel, n), out_shape=(cache, c...  32.1 us
    unnamed x28, local copies, waits for them, and re-layouts  12.2 us

profile of v1, /device:TPU:0, one launch (start us, length us, event | category | flops | bytes accessed | tf_op | source)
XLA Modules:
  0.0 185.9 jit_solution(14673951318689130106)
XLA Ops:
  0.6 0.7 pad_add_fusion
  1.4 1.1 reshape.23
  2.6 0.0 copy-start
  2.6 1.6 copy-done
  4.1 0.0 copy-start.1
  4.1 1.6 copy-done.1
  5.7 0.0 copy-start.8
  5.7 0.8 copy-done.8
  6.5 0.0 copy-start.9
  6.5 0.8 copy-done.9
  7.3 0.0 copy-start.11
  7.3 0.7 copy-done.11
  7.9 0.0 copy-start.12
  7.9 0.7 copy-done.12
  8.6 0.0 copy-start.13
  8.6 0.7 copy-done.13
  9.2 32.1 %exchange.1 = (bf16[32,128,256]{2,1,0:T(8,128)(2,1)S(1)}, bf16[32,128,256]{2,1,0:T(8,128)(2,1)S(1)}, bf16[32,32,128]{2,1,0:T(8,128)(2,1)S(1)}, bf16[7,2,128,256]...) custom-call(s32[32]{0:T(128)S(1)} %copy-done.11, s32[1,4]{1,0:T(1,128)S(1)} %copy-done.12, ...), custom_call_target="tpu_custom_call" | custom-call | tf_op jit(solution)/shard_map/exchange/pallas_call | solution.py:269
  41.3 0.0 copy-start.2
  41.4 1.3 copy-done.2
  42.7 0.0 copy-start.3
  42.7 1.3 copy-done.3
  44.0 0.0 copy-start.4
  44.0 0.9 copy-done.4
  44.9 0.0 copy-start.5
  44.9 0.7 copy-done.5
  45.7 0.0 copy-start.7
  45.7 0.6 copy-done.7
  46.3 0.0 copy-start.10
  46.3 0.6 copy-done.10
  46.9 0.0 copy-start.6
  46.9 137.3 %place.1 = (bf16[32,128,256]{2,1,0:T(8,128)(2,1)}, bf16[32,128,256]{2,1,0:T(8,128)(2,1)}, bf16[32,32,128]{2,1,0:T(8,128)(2,1)}) custom-call(s32[1]{0:T(128)} %bitcast.3.me_ref, s32[7,1,128]{2,1,0:T(1,128)} %copy-done.10, bf16[32,128,256]{2,1,0:T(8,128)(2,1)} %copy-done.2, bf16[32,128,256]{2,1,0:T(8,128)(2,1)} %copy-done.3, bf16[32,32,128]{2,1,0:T(8,128)(2,1)} %copy-done.5, ...), custom_call_target="tpu_custom_call" | custom-call | tf_op jit(solution)/shard_map/place/pallas_call | solution.py:298
  184.2 0.9 slice.9
  185.1 0.0 copy-done.6
  185.1 0.8 copy_bitcast_fusion
  (3 shorter events, 0.1 us)
Async XLA Ops:
  2.6 1.6 copy-start
  4.1 1.6 copy-start.1
  5.7 0.8 copy-start.8
  6.5 0.8 copy-start.9
  7.3 0.7 copy-start.11
  7.9 0.7 copy-start.12
  8.6 0.7 copy-start.13
  41.3 1.3 copy-start.2
  42.7 1.3 copy-start.3
  44.0 0.9 copy-start.4
  44.9 0.7 copy-start.5
  45.7 0.6 copy-start.7
  46.3 0.6 copy-start.10
  46.9 138.3 %copy-start.6 = (bf16[32,32,128]{2,1,0:T(8,128)(2,1)S(1)}, bf16[32,32,128]{2,1,0:T(8,128)(2,1)}, u32[]{:S(2)}) copy-start(bf16[32,32,128]{2,1,0:T(8,128)(2,1)} %copy-done.5) | copy-start | bytes 786436

commit v2 on v1

v2 whole, which is shorter than its diff:
```python
import functools

import jax
import jax.numpy as jnp
from jax import lax
from jax.experimental import pallas as pl
from jax.experimental.pallas import tpu as pltpu
from jax.sharding import PartitionSpec as P

HS = 128
MASKED = -1e30
MESH = pl.DeviceIdType.MESH
TILE = 8
UNROLL = 4


def written(cached, fresh, size, place):
    fresh = fresh.astype(jnp.float32)
    cached = cached.astype(jnp.float32)
    out = jnp.where(place < size, cached, 0.0)
    out = jnp.where(place == size, fresh[0:1], out)
    out = jnp.where(place == size + 1, fresh[1:2], out)
    return out.astype(jnp.bfloat16)


def exchange_kernel(
    n,
    lens_hbm,
    move_rows_hbm,
    move_targets_hbm,
    move_landing_hbm,
    q_hbm,
    fk_hbm,
    fv_hbm,
    ck_hbm,
    cv_hbm,
    nk,
    nv,
    first_out,
    second_out,
    got,
    got_o,
    got_targets,
    got_landing,
    lens,
    move_rows,
    move_targets,
    q,
    fk,
    fv,
    ck,
    cv,
    first_o,
    second_o,
    second_rows,
    pack,
    pack_o,
    in_sem,
    out_sem,
    send_sem,
    recv_sem,
):
    me = lax.axis_index("inst")
    rows, ctx, width = ck.shape
    heads = width // HS
    group = q.shape[2] // width
    moves = move_rows.shape[1]

    loads = [
        pltpu.make_async_copy(src, dst, in_sem.at[i])
        for i, (src, dst) in enumerate(
            (
                (lens_hbm, lens),
                (move_rows_hbm, move_rows),
                (move_targets_hbm, move_targets),
                (fk_hbm, fk),
                (fv_hbm, fv),
                (ck_hbm, ck),
                (cv_hbm, cv),
                (q_hbm, q),
            )
        )
    ]
    for load in loads:
        load.start()

    barrier = pltpu.get_barrier_semaphore()
    for d in range(1, n):
        pl.semaphore_signal(
            barrier, inc=1, device_id={"inst": lax.rem(me + d, n)}, device_id_type=MESH
        )

    place = lax.broadcasted_iota(jnp.int32, (ctx, width), 0)

    def leaving(peer):
        row = jnp.int32(0)
        for j in range(moves):
            row = row + jnp.where(move_targets[0, j] == peer, move_rows[0, j], 0)
        return row

    def remote(src, dst, part, d):
        return pltpu.make_async_remote_copy(
            src_ref=src,
            dst_ref=dst,
            send_sem=send_sem.at[part, d - 1],
            recv_sem=recv_sem.at[part, d - 1],
            device_id={"inst": lax.rem(me + d, n)},
            device_id_type=MESH,
        )

    def send_k(d):
        return remote(pack.at[d - 1, 0], got.at[d - 1, 0], 0, d)

    def send_v(d):
        return remote(pack.at[d - 1, 1], got.at[d - 1, 1], 1, d)

    def send_o(d):
        return remote(pack_o.at[d - 1], got_o.at[d - 1], 2, d)

    def send_targets(d):
        return remote(move_targets_hbm, got_targets.at[d - 1], 3, d)

    def send_landing(d):
        return remote(move_landing_hbm, got_landing.at[d - 1], 4, d)

    for load in loads[:6]:
        load.wait()
    pl.semaphore_wait(barrier, n - 1)

    @pl.loop(1, n)
    def _(d):
        row = leaving(lax.rem(me + d, n))
        pack[d - 1, 0] = written(ck[row], fk[row], lens[row], place)
        send_k(d).start()

    loads[6].wait()

    @pl.loop(1, n)
    def _(d):
        row = leaving(lax.rem(me + d, n))
        pack[d - 1, 1] = written(cv[row], fv[row], lens[row], place)
        send_v(d).start()

    @pl.loop(1, n)
    def _(d):
        send_targets(d).start()
        send_landing(d).start()

    loads[7].wait()
    qrows = 2 * group
    offset = lax.broadcasted_iota(jnp.int32, (qrows, ctx), 1) - lax.rem(
        lax.broadcasted_iota(jnp.int32, (qrows, ctx), 0), 2
    )
    scale = HS ** (-0.5)

    def save_k(first):
        return pltpu.make_async_copy(
            ck.at[pl.ds(first, UNROLL)], nk.at[pl.ds(first, UNROLL)], out_sem.at[0]
        )

    def save_v(first):
        return pltpu.make_async_copy(
            cv.at[pl.ds(first, UNROLL)], nv.at[pl.ds(first, UNROLL)], out_sem.at[1]
        )

    def work(block, low):
        first = block * TILE + low
        values = []
        scores = []
        for u in range(UNROLL):
            r = first + u
            size = lens[r]
            keys = written(ck[r], fk[r], size, place)
            vals = written(cv[r], fv[r], size, place)
            ck[r] = keys
            cv[r] = vals
            values.append(vals)
            query = q[r].astype(jnp.float32)
            for h in range(heads):
                at = h * group
                rows_of = jnp.concatenate(
                    [query[:, (at + g) * HS : (at + g + 1) * HS] for g in range(group)], axis=0
                )
                s = lax.dot_general(
                    rows_of.astype(jnp.bfloat16),
                    keys[:, h * HS : (h + 1) * HS],
                    (((1,), (1,)), ((), ())),
                    preferred_element_type=jnp.float32,
                )
                scores.append(jnp.where(offset <= size, s * scale, MASKED))
        save_k(first).start()
        save_v(first).start()
        s = jnp.concatenate(scores, axis=0)
        w = jnp.exp(s - jnp.max(s, axis=1, keepdims=True))
        totals = jnp.sum(w, axis=1, keepdims=True)
        w = w.astype(jnp.bfloat16)
        for u in range(UNROLL):
            for h in range(heads):
                at = (u * heads + h) * qrows
                mixed = lax.dot_general(
                    w[at : at + qrows],
                    values[u][:, h * HS : (h + 1) * HS],
                    (((1,), (0,)), ((), ())),
                    preferred_element_type=jnp.float32,
                )
                mixed = mixed / totals[at : at + qrows]
                for g in range(group):
                    lanes = pl.ds((h * group + g) * HS, HS)
                    second = mixed[2 * g + 1 : 2 * g + 2]
                    first_o[block, low + u : low + u + 1, lanes] = mixed[2 * g : 2 * g + 1]
                    second_o[block, low + u : low + u + 1, lanes] = second
                    second_rows[first + u, :, lanes] = second

    @pl.loop(0, rows // TILE)
    def _(block):
        for first in range(0, TILE, UNROLL):
            work(block, first)

    saves = [
        pltpu.make_async_copy(first_o, first_out, out_sem.at[2]),
        pltpu.make_async_copy(second_o, second_out, out_sem.at[3]),
    ]
    for save in saves:
        save.start()

    @pl.loop(1, n)
    def _(d):
        row = leaving(lax.rem(me + d, n))
        pack_o[d - 1] = second_rows[row]
        send_o(d).start()

    for save in saves:
        save.wait()
    pltpu.make_async_copy(ck, nk, out_sem.at[0]).wait()
    pltpu.make_async_copy(cv, nv, out_sem.at[1]).wait()

    @pl.loop(1, n)
    def _(d):
        send_targets(d).wait()
        send_landing(d).wait()
        send_k(d).wait()
        send_v(d).wait()
        send_o(d).wait()


def place_kernel(
    n,
    targets_hbm,
    landing_hbm,
    move_rows_hbm,
    nk,
    nv,
    first_hbm,
    second_hbm,
    got,
    got_o,
    out_first,
    out_second,
    out_k,
    out_v,
    targets,
    landing,
    move_rows,
    moved,
    dest,
    k,
    v,
    first,
    second,
    land,
    land_o,
    first_b,
    second_b,
    in_sem,
    chunk_sem,
    land_sem,
    out_sem,
):
    rows = nk.shape[0]
    moves = move_rows.shape[1]
    me = lax.axis_index("inst")
    chunks = chunk_sem.shape[1]
    size = rows // chunks
    small = [
        pltpu.make_async_copy(src, dst, in_sem.at[i])
        for i, (src, dst) in enumerate(
            (
                (move_rows_hbm, move_rows),
                (targets_hbm, targets),
                (landing_hbm, landing),
                (first_hbm, first),
                (second_hbm, second),
            )
        )
    ]
    for copy in small[:3]:
        copy.start()

    def load(c):
        part = pl.ds(c * size, size)
        return (
            pltpu.make_async_copy(nk.at[part], k.at[part], chunk_sem.at[0, c]),
            pltpu.make_async_copy(nv.at[part], v.at[part], chunk_sem.at[1, c]),
        )

    for c in range(chunks):
        for copy in load(c):
            copy.start()
    for copy in small[3:]:
        copy.start()

    @pl.loop(0, rows)
    def _(s):
        moved[s] = 0

    for copy in small[:3]:
        copy.wait()
    for j in range(moves):
        moved[move_rows[0, j]] = 1

    def arrive(d, count):
        row = jnp.int32(0)
        found = jnp.int32(0)
        for j in range(moves):
            mine = targets[d, 0, j] == me
            row = row + jnp.where(mine, landing[d, 0, j], 0)
            found = found + jnp.where(mine, 1, 0)

        @pl.when(found > 0)
        def _():
            dest[count] = row
            pltpu.make_async_copy(got.at[d], land.at[count], land_sem.at[0]).start()
            pltpu.make_async_copy(got_o.at[d], land_o.at[count], land_sem.at[1]).start()

        return count + found

    lax.fori_loop(0, n - 1, arrive, jnp.int32(0))

    for c in range(chunks):
        for copy in load(c):
            copy.wait()

        @pl.loop(c * size, (c + 1) * size)
        def _(s):
            @pl.when(moved[s] == 0)
            def _():
                pltpu.make_async_copy(k.at[s], out_k.at[s], out_sem.at[0]).start()
                pltpu.make_async_copy(v.at[s], out_v.at[s], out_sem.at[1]).start()

    pltpu.make_async_copy(got.at[pl.ds(0, moves)], land, land_sem.at[0]).wait()
    for j in range(moves):
        pltpu.make_async_copy(land.at[j, 0], out_k.at[dest[j]], out_sem.at[0]).start()
        pltpu.make_async_copy(land.at[j, 1], out_v.at[dest[j]], out_sem.at[1]).start()
    for copy in small[3:]:
        copy.wait()
    first_b[...] = first[...].astype(jnp.bfloat16)
    save_first = pltpu.make_async_copy(first_b, out_first, out_sem.at[2])
    save_first.start()
    pltpu.make_async_copy(got_o.at[pl.ds(0, moves)], land_o, land_sem.at[1]).wait()
    settled = second[...]
    slot = lax.broadcasted_iota(jnp.int32, settled.shape, 0)
    for j in range(moves):
        settled = jnp.where(slot == dest[j], land_o[j], settled)
    second_b[...] = settled.astype(jnp.bfloat16)
    save_second = pltpu.make_async_copy(second_b, out_second, out_sem.at[3])
    save_second.start()
    save_first.wait()
    save_second.wait()
    pltpu.make_async_copy(k, out_k, out_sem.at[0]).wait()
    pltpu.make_async_copy(v, out_v, out_sem.at[1]).wait()


def on_device(
    n,
    queries,
    fresh_keys,
    fresh_values,
    cache_keys,
    cache_values,
    lengths,
    move_rows,
    move_targets,
    move_landing,
):
    rows, ctx, width = cache_keys.shape
    wide = queries.shape[2]
    moves = move_rows.shape[1]
    chunks = 4
    tiled = (rows // TILE, TILE, wide)
    bf16, f32, i32 = jnp.bfloat16, jnp.float32, jnp.int32
    hbm = pl.BlockSpec(memory_space=pltpu.HBM)
    shape = jax.ShapeDtypeStruct
    cache = shape((rows, ctx, width), bf16)
    nk, nv, first, second, got, got_o, targets, landing = pl.pallas_call(
        functools.partial(exchange_kernel, n),
        out_shape=(
            cache,
            cache,
            shape(tiled, f32),
            shape(tiled, f32),
            shape((n - 1, 2, ctx, width), bf16),
            shape((n - 1, 1, wide), f32),
            shape((n - 1, 1, moves), i32),
            shape((n - 1, 1, moves), i32),
        ),
        in_specs=[hbm] * 9,
        out_specs=(hbm,) * 8,
        scratch_shapes=[
            pltpu.SMEM((rows,), i32),
            pltpu.SMEM((1, moves), i32),
            pltpu.SMEM((1, moves), i32),
            pltpu.VMEM(queries.shape, bf16),
            pltpu.VMEM(fresh_keys.shape, bf16),
            pltpu.VMEM(fresh_keys.shape, bf16),
            pltpu.VMEM((rows, ctx, width), bf16),
            pltpu.VMEM((rows, ctx, width), bf16),
            pltpu.VMEM(tiled, f32),
            pltpu.VMEM(tiled, f32),
            pltpu.VMEM((rows, 1, wide), f32),
            pltpu.VMEM((n - 1, 2, ctx, width), bf16),
            pltpu.VMEM((n - 1, 1, wide), f32),
            pltpu.SemaphoreType.DMA((8,)),
            pltpu.SemaphoreType.DMA((4,)),
            pltpu.SemaphoreType.DMA((5, n - 1)),
            pltpu.SemaphoreType.DMA((5, n - 1)),
        ],
        compiler_params=pltpu.CompilerParams(
            collective_id=0, has_side_effects=True, vmem_limit_bytes=48 * 2**20
        ),
        name="exchange",
    )(
        lengths,
        move_rows,
        move_targets,
        move_landing,
        queries,
        fresh_keys,
        fresh_values,
        cache_keys,
        cache_values,
    )
    return pl.pallas_call(
        functools.partial(place_kernel, n),
        out_shape=(shape((rows, wide), bf16), shape((rows, wide), bf16), cache, cache),
        in_specs=[hbm] * 9,
        out_specs=(hbm,) * 4,
        scratch_shapes=[
            pltpu.SMEM((n - 1, 1, moves), i32),
            pltpu.SMEM((n - 1, 1, moves), i32),
            pltpu.SMEM((1, moves), i32),
            pltpu.SMEM((rows,), i32),
            pltpu.SMEM((rows,), i32),
            pltpu.VMEM((rows, ctx, width), bf16),
            pltpu.VMEM((rows, ctx, width), bf16),
            pltpu.VMEM((rows, wide), f32),
            pltpu.VMEM((rows, wide), f32),
            pltpu.VMEM((moves, 2, ctx, width), bf16),
            pltpu.VMEM((moves, 1, wide), f32),
            pltpu.VMEM((rows, wide), bf16),
            pltpu.VMEM((rows, wide), bf16),
            pltpu.SemaphoreType.DMA((5,)),
            pltpu.SemaphoreType.DMA((2, chunks)),
            pltpu.SemaphoreType.DMA((2,)),
            pltpu.SemaphoreType.DMA((4,)),
        ],
        compiler_params=pltpu.CompilerParams(vmem_limit_bytes=48 * 2**20),
        name="place",
    )(
        targets,
        landing,
        move_rows,
        nk,
        nv,
        first.reshape(rows, wide),
        second.reshape(rows, wide),
        got,
        got_o,
    )


def solution(mesh):
    split = P(("groups", "inst"), None, "tp")
    table = P(("groups", "inst"), None)
    return jax.shard_map(
        functools.partial(on_device, mesh.shape["inst"]),
        mesh=mesh,
        in_specs=(split,) * 5 + (P(("groups", "inst")), table, table, table),
        out_specs=(P(("groups", "inst"), "tp"), P(("groups", "inst"), "tp"), split, split),
        check_vma=False,
    )
```

time: 186 us -> 41.9 us (0.23)
  Pallas kernels: 169 us -> 35.8 us
  local copies, waits for them, and re-layouts: 15 us -> 5.08 us
    pallas_call x1, Pallas kernels: 137 us -> 3.74 us  [on_device(): pl.pallas_call(functools.partial(place_kernel, n), out_shape=(shape((rows...]
    unnamed x28 -> x14, local copies, waits for them, and re-layouts: 12.2 us -> 5.08 us
where the time goes in v2:
time: 41.9 us; the launch traced here: 41.5 us
  Pallas kernels  35.8 us (85%)
  local copies, waits for them, and re-layouts  5.08 us (12%)
  between operations  0.66 us (2%)
    pallas_call x1, Pallas kernels, on_device(): pl.pallas_call(functools.partial(exchange_kernel, n), out_shape=(cache, c...  32.1 us
    unnamed x14, local copies, waits for them, and re-layouts  5.08 us
    pallas_call x1, Pallas kernels, on_device(): pl.pallas_call(functools.partial(place_kernel, n), out_shape=(shape((rows...  3.74 us

profile of v2, /device:TPU:0, one launch (start us, length us, event | category | flops | bytes accessed | tf_op | source)
XLA Modules:
  0.0 41.5 jit_solution(6804906721854571207)
XLA Ops:
  0.6 0.0 copy-start
  0.6 0.9 %copy-done = bf16[32,2,2048]{2,1,0:T(2,128)(2,1)S(1)} copy-done((bf16[32,2,2048]{2,1,0:T(2,128)(2,1)S(1)}, bf16[32,2,2048]{2,1,0:T(2,128)(2,1)}, u32[]{:S(2)}) %copy-start) | copy-done | bytes 262168
  1.6 0.0 copy-start.1
  1.6 0.8 %copy-done.1 = bf16[32,2,256]{2,1,0:T(2,128)(2,1)S(1)} copy-done((bf16[32,2,256]{2,1,0:T(2,128)(2,1)S(1)}, bf16[32,2,256]{2,1,0:T(2,128)(2,1)}, u32[]{:S(2)}) %copy-start.1) | copy-done | bytes 32792
  2.3 0.0 copy-start.2
  2.3 0.8 %copy-done.2 = bf16[32,2,256]{2,1,0:T(2,128)(2,1)S(1)} copy-done((bf16[32,2,256]{2,1,0:T(2,128)(2,1)S(1)}, bf16[32,2,256]{2,1,0:T(2,128)(2,1)}, u32[]{:S(2)}) %copy-start.2) | copy-done | bytes 32792
  3.1 0.0 copy-start.3
  3.1 0.7 %copy-done.3 = s32[1,4]{1,0:T(1,128)S(1)} copy-done((s32[1,4]{1,0:T(1,128)S(1)}, s32[1,4]{1,0:T(1,128)}, u32[]{:S(2)}) %copy-start.3) | copy-done | bytes 40
  3.8 0.0 copy-start.4
  3.8 0.7 %copy-done.4 = s32[32]{0:T(128)S(1)} copy-done((s32[32]{0:T(128)S(1)}, s32[32]{0:T(128)}, u32[]{:S(2)}) %copy-start.4) | copy-done | bytes 152
  4.4 0.0 copy-start.5
  4.4 0.7 %copy-done.5 = s32[1,4]{1,0:T(1,128)S(1)} copy-done((s32[1,4]{1,0:T(1,128)S(1)}, s32[1,4]{1,0:T(1,128)}, u32[]{:S(2)}) %copy-start.5) | copy-done | bytes 40
  5.1 0.0 copy-start.6
  5.1 0.7 %copy-done.6 = s32[1,4]{1,0:T(1,128)S(1)} copy-done((s32[1,4]{1,0:T(1,128)S(1)}, s32[1,4]{1,0:T(1,128)}, u32[]{:S(2)}) %copy-start.6) | copy-done | bytes 40
  5.7 32.1 %exchange.1 = (bf16[32,128,256]{2,1,0:T(8,128)(2,1)S(1)}, bf16[32,128,256]{2,1,0:T(8,128)(2,1)S(1)}, f32[4,8,2048]{2,1,0:T(8,128)S(1)}, f32[4,8,2048]{2,1,0:T(8,...) custom-call(s32[32]{0:T(128)S(1)} %copy-done.4, ...), custom_call_target="tpu_custom_call" | custom-call | tf_op jit(solution)/shard_map/exchange/pallas_call | solution.py:394
  37.8 3.7 %place.1 = (bf16[32,2048]{1,0:T(8,128)(2,1)}, bf16[32,2048]{1,0:T(8,128)(2,1)}, bf16[32,128,256]{2,1,0:T(8,128)(2,1)}, bf16[32,128,256]{2,1,0:T(8,128)(2,1)}) custom-call(s32[7,1,4]{2,1,0:T(1,128)S(1)} %get-tuple-element.12.targets_hbm, s32[7,1,4]{2,1,0:T(1,128)S(1)} %get-tuple-element.13.landing_hbm, s32[1,4]{1,0:T(1,128)S(1)} %copy-done.3, ...), custom_call_target="tpu_custom_call" | custom-call | tf_op jit(solution)/shard_map/place/pallas_call | solution.py:442
Async XLA Ops:
  0.6 1.0 %copy-start = (bf16[32,2,2048]{2,1,0:T(2,128)(2,1)S(1)}, bf16[32,2,2048]{2,1,0:T(2,128)(2,1)}, u32[]{:S(2)}) copy-start(bf16[32,2,2048]{2,1,0:T(2,128)(2,1)} %q_hbm.1) | copy-start | bytes 786436
  1.6 0.8 %copy-start.1 = (bf16[32,2,256]{2,1,0:T(2,128)(2,1)S(1)}, bf16[32,2,256]{2,1,0:T(2,128)(2,1)}, u32[]{:S(2)}) copy-start(bf16[32,2,256]{2,1,0:T(2,128)(2,1)} %fk_hbm.1) | copy-start | bytes 98308
  2.3 0.8 %copy-start.2 = (bf16[32,2,256]{2,1,0:T(2,128)(2,1)S(1)}, bf16[32,2,256]{2,1,0:T(2,128)(2,1)}, u32[]{:S(2)}) copy-start(bf16[32,2,256]{2,1,0:T(2,128)(2,1)} %fv_hbm.1) | copy-start | bytes 98308
  3.1 0.7 %copy-start.3 = (s32[1,4]{1,0:T(1,128)S(1)}, s32[1,4]{1,0:T(1,128)}, u32[]{:S(2)}) copy-start(s32[1,4]{1,0:T(1,128)} %move_rows_hbm.3) | copy-start | bytes 52
  3.8 0.7 %copy-start.4 = (s32[32]{0:T(128)S(1)}, s32[32]{0:T(128)}, u32[]{:S(2)}) copy-start(s32[32]{0:T(128)} %lens_hbm.1) | copy-start | bytes 388
  4.4 0.7 %copy-start.5 = (s32[1,4]{1,0:T(1,128)S(1)}, s32[1,4]{1,0:T(1,128)}, u32[]{:S(2)}) copy-start(s32[1,4]{1,0:T(1,128)} %move_targets_hbm.1) | copy-start | bytes 52
  5.1 0.7 %copy-start.6 = (s32[1,4]{1,0:T(1,128)S(1)}, s32[1,4]{1,0:T(1,128)}, u32[]{:S(2)}) copy-start(s32[1,4]{1,0:T(1,128)} %move_landing_hbm.1) | copy-start | bytes 52

commit v3 on v2

--- a/solution.py
+++ b/solution.py
@@ -36,8 +36,8 @@
     cv_hbm,
     nk,
     nv,
-    first_out,
-    second_out,
+    first_o,
+    second_o,
     got,
     got_o,
     got_targets,
@@ -50,13 +50,10 @@
     fv,
     ck,
     cv,
-    first_o,
-    second_o,
     second_rows,
     pack,
     pack_o,
     in_sem,
-    out_sem,
     send_sem,
     recv_sem,
 ):
@@ -81,7 +78,7 @@
             )
         )
     ]
-    for load in loads:
+    for load in loads[:6]:
         load.start()
 
     barrier = pltpu.get_barrier_semaphore()
@@ -125,6 +122,8 @@
 
     for load in loads[:6]:
         load.wait()
+    for load in loads[6:]:
+        load.start()
     pl.semaphore_wait(barrier, n - 1)
 
     @pl.loop(1, n)
@@ -152,16 +151,6 @@
         lax.broadcasted_iota(jnp.int32, (qrows, ctx), 0), 2
     )
     scale = HS ** (-0.5)
-
-    def save_k(first):
-        return pltpu.make_async_copy(
-            ck.at[pl.ds(first, UNROLL)], nk.at[pl.ds(first, UNROLL)], out_sem.at[0]
-        )
-
-    def save_v(first):
-        return pltpu.make_async_copy(
-            cv.at[pl.ds(first, UNROLL)], nv.at[pl.ds(first, UNROLL)], out_sem.at[1]
-        )
 
     def work(block, low):
         first = block * TILE + low
@@ -172,8 +161,8 @@
             size = lens[r]
             keys = written(ck[r], fk[r], size, place)
             vals = written(cv[r], fv[r], size, place)
-            ck[r] = keys
-            cv[r] = vals
+            nk[r] = keys
+            nv[r] = vals
             values.append(vals)
             query = q[r].astype(jnp.float32)
             for h in range(heads):
@@ -188,8 +177,6 @@
                     preferred_element_type=jnp.float32,
                 )
                 scores.append(jnp.where(offset <= size, s * scale, MASKED))
-        save_k(first).start()
-        save_v(first).start()
         s = jnp.concatenate(scores, axis=0)
         w = jnp.exp(s - jnp.max(s, axis=1, keepdims=True))
         totals = jnp.sum(w, axis=1, keepdims=True)
@@ -216,23 +203,11 @@
         for first in range(0, TILE, UNROLL):
             work(block, first)
 
-    saves = [
-        pltpu.make_async_copy(first_o, first_out, out_sem.at[2]),
-        pltpu.make_async_copy(second_o, second_out, out_sem.at[3]),
-    ]
-    for save in saves:
-        save.start()
-
     @pl.loop(1, n)
     def _(d):
         row = leaving(lax.rem(me + d, n))
         pack_o[d - 1] = second_rows[row]
         send_o(d).start()
-
-    for save in saves:
-        save.wait()
-    pltpu.make_async_copy(ck, nk, out_sem.at[0]).wait()
-    pltpu.make_async_copy(cv, nv, out_sem.at[1]).wait()
 
     @pl.loop(1, n)
     def _(d):
@@ -250,8 +225,8 @@
     move_rows_hbm,
     nk,
     nv,
-    first_hbm,
-    second_hbm,
+    first,
+    second,
     got,
     got_o,
     out_first,
@@ -263,24 +238,15 @@
     move_rows,
     moved,
     dest,
-    k,
-    v,
-    first,
-    second,
-    land,
-    land_o,
+    origin,
     first_b,
     second_b,
     in_sem,
-    chunk_sem,
-    land_sem,
     out_sem,
 ):
     rows = nk.shape[0]
     moves = move_rows.shape[1]
     me = lax.axis_index("inst")
-    chunks = chunk_sem.shape[1]
-    size = rows // chunks
     small = [
         pltpu.make_async_copy(src, dst, in_sem.at[i])
         for i, (src, dst) in enumerate(
@@ -288,35 +254,31 @@
                 (move_rows_hbm, move_rows),
                 (targets_hbm, targets),
                 (landing_hbm, landing),
-                (first_hbm, first),
-                (second_hbm, second),
             )
         )
     ]
-    for copy in small[:3]:
+    for copy in small:
         copy.start()
 
-    def load(c):
-        part = pl.ds(c * size, size)
-        return (
-            pltpu.make_async_copy(nk.at[part], k.at[part], chunk_sem.at[0, c]),
-            pltpu.make_async_copy(nv.at[part], v.at[part], chunk_sem.at[1, c]),
-        )
-
-    for c in range(chunks):
-        for copy in load(c):
-            copy.start()
-    for copy in small[3:]:
-        copy.start()
+    first_b[...] = first[...].astype(jnp.bfloat16)
+    save_first = pltpu.make_async_copy(first_b, out_first, out_sem.at[2])
+    save_first.start()
 
     @pl.loop(0, rows)
     def _(s):
         moved[s] = 0
 
-    for copy in small[:3]:
+    for copy in small:
         copy.wait()
     for j in range(moves):
         moved[move_rows[0, j]] = 1
+
+    @pl.loop(0, rows)
+    def _(s):
+        @pl.when(moved[s] == 0)
+        def _():
+            pltpu.make_async_copy(nk.at[s], out_k.at[s], out_sem.at[0]).start()
+            pltpu.make_async_copy(nv.at[s], out_v.at[s], out_sem.at[1]).start()
 
     def arrive(d, count):
         row = jnp.int32(0)
@@ -329,45 +291,24 @@
         @pl.when(found > 0)
         def _():
             dest[count] = row
-            pltpu.make_async_copy(got.at[d], land.at[count], land_sem.at[0]).start()
-            pltpu.make_async_copy(got_o.at[d], land_o.at[count], land_sem.at[1]).start()
+            origin[count] = d
+            pltpu.make_async_copy(got.at[d, 0], out_k.at[row], out_sem.at[0]).start()
+            pltpu.make_async_copy(got.at[d, 1], out_v.at[row], out_sem.at[1]).start()
 
         return count + found
 
     lax.fori_loop(0, n - 1, arrive, jnp.int32(0))
-
-    for c in range(chunks):
-        for copy in load(c):
-            copy.wait()
-
-        @pl.loop(c * size, (c + 1) * size)
-        def _(s):
-            @pl.when(moved[s] == 0)
-            def _():
-                pltpu.make_async_copy(k.at[s], out_k.at[s], out_sem.at[0]).start()
-                pltpu.make_async_copy(v.at[s], out_v.at[s], out_sem.at[1]).start()
-
-    pltpu.make_async_copy(got.at[pl.ds(0, moves)], land, land_sem.at[0]).wait()
-    for j in range(moves):
-        pltpu.make_async_copy(land.at[j, 0], out_k.at[dest[j]], out_sem.at[0]).start()
-        pltpu.make_async_copy(land.at[j, 1], out_v.at[dest[j]], out_sem.at[1]).start()
-    for copy in small[3:]:
-        copy.wait()
-    first_b[...] = first[...].astype(jnp.bfloat16)
-    save_first = pltpu.make_async_copy(first_b, out_first, out_sem.at[2])
-    save_first.start()
-    pltpu.make_async_copy(got_o.at[pl.ds(0, moves)], land_o, land_sem.at[1]).wait()
     settled = second[...]
     slot = lax.broadcasted_iota(jnp.int32, settled.shape, 0)
     for j in range(moves):
-        settled = jnp.where(slot == dest[j], land_o[j], settled)
+        settled = jnp.where(slot == dest[j], got_o[origin[j]], settled)
     second_b[...] = settled.astype(jnp.bfloat16)
     save_second = pltpu.make_async_copy(second_b, out_second, out_sem.at[3])
     save_second.start()
     save_first.wait()
     save_second.wait()
-    pltpu.make_async_copy(k, out_k, out_sem.at[0]).wait()
-    pltpu.make_async_copy(v, out_v, out_sem.at[1]).wait()
+    pltpu.make_async_copy(nk, out_k, out_sem.at[0]).wait()
+    pltpu.make_async_copy(nv, out_v, out_sem.at[1]).wait()
 
 
 def on_device(
@@ -385,26 +326,26 @@
     rows, ctx, width = cache_keys.shape
     wide = queries.shape[2]
     moves = move_rows.shape[1]
-    chunks = 4
     tiled = (rows // TILE, TILE, wide)
     bf16, f32, i32 = jnp.bfloat16, jnp.float32, jnp.int32
     hbm = pl.BlockSpec(memory_space=pltpu.HBM)
+    vmem = pl.BlockSpec(memory_space=pltpu.VMEM)
     shape = jax.ShapeDtypeStruct
     cache = shape((rows, ctx, width), bf16)
     nk, nv, first, second, got, got_o, targets, landing = pl.pallas_call(
         functools.partial(exchange_kernel, n),
         out_shape=(
-            cache,
-            cache,
-            shape(tiled, f32),
-            shape(tiled, f32),
-            shape((n - 1, 2, ctx, width), bf16),
-            shape((n - 1, 1, wide), f32),
-            shape((n - 1, 1, moves), i32),
-            shape((n - 1, 1, moves), i32),
+            pltpu.VMEM((rows, ctx, width), bf16),
+            pltpu.VMEM((rows, ctx, width), bf16),
+            pltpu.VMEM(tiled, f32),
+            pltpu.VMEM(tiled, f32),
+            pltpu.VMEM((n - 1, 2, ctx, width), bf16),
+            pltpu.VMEM((n - 1, 1, wide), f32),
+            pltpu.VMEM((n - 1, 1, moves), i32),
+            pltpu.VMEM((n - 1, 1, moves), i32),
         ),
         in_specs=[hbm] * 9,
-        out_specs=(hbm,) * 8,
+        out_specs=(vmem,) * 8,
         scratch_shapes=[
             pltpu.SMEM((rows,), i32),
             pltpu.SMEM((1, moves), i32),
@@ -414,35 +355,37 @@
             pltpu.VMEM(fresh_keys.shape, bf16),
             pltpu.VMEM((rows, ctx, width), bf16),
             pltpu.VMEM((rows, ctx, width), bf16),
-            pltpu.VMEM(tiled, f32),
-            pltpu.VMEM(tiled, f32),
             pltpu.VMEM((rows, 1, wide), f32),
             pltpu.VMEM((n - 1, 2, ctx, width), bf16),
             pltpu.VMEM((n - 1, 1, wide), f32),
             pltpu.SemaphoreType.DMA((8,)),
-            pltpu.SemaphoreType.DMA((4,)),
             pltpu.SemaphoreType.DMA((5, n - 1)),
             pltpu.SemaphoreType.DMA((5, n - 1)),
         ],
         compiler_params=pltpu.CompilerParams(
-            collective_id=0, has_side_effects=True, vmem_limit_bytes=48 * 2**20
+            collective_id=0, has_side_effects=True, vmem_limit_bytes=32 * 2**20
         ),
         name="exchange",
     )(
-        lengths,
-        move_rows,
-        move_targets,
-        move_landing,
-        queries,
-        fresh_keys,
-        fresh_values,
-        cache_keys,
-        cache_values,
+        *(
+            pltpu.with_memory_space_constraint(x, pltpu.HBM)
+            for x in (
+                lengths,
+                move_rows,
+                move_targets,
+                move_landing,
+                queries,
+                fresh_keys,
+                fresh_values,
+                cache_keys,
+                cache_values,
+            )
+        )
     )
     return pl.pallas_call(
         functools.partial(place_kernel, n),
         out_shape=(shape((rows, wide), bf16), shape((rows, wide), bf16), cache, cache),
-        in_specs=[hbm] * 9,
+        in_specs=[vmem, vmem, hbm] + [vmem] * 6,
         out_specs=(hbm,) * 4,
         scratch_shapes=[
             pltpu.SMEM((n - 1, 1, moves), i32),
@@ -450,20 +393,13 @@
             pltpu.SMEM((1, moves), i32),
             pltpu.SMEM((rows,), i32),
             pltpu.SMEM((rows,), i32),
-            pltpu.VMEM((rows, ctx, width), bf16),
-            pltpu.VMEM((rows, ctx, width), bf16),
-            pltpu.VMEM((rows, wide), f32),
-            pltpu.VMEM((rows, wide), f32),
-            pltpu.VMEM((moves, 2, ctx, width), bf16),
-            pltpu.VMEM((moves, 1, wide), f32),
+            pltpu.SMEM((rows,), i32),
             pltpu.VMEM((rows, wide), bf16),
             pltpu.VMEM((rows, wide), bf16),
-            pltpu.SemaphoreType.DMA((5,)),
-            pltpu.SemaphoreType.DMA((2, chunks)),
-            pltpu.SemaphoreType.DMA((2,)),
+            pltpu.SemaphoreType.DMA((3,)),
             pltpu.SemaphoreType.DMA((4,)),
         ],
-        compiler_params=pltpu.CompilerParams(vmem_limit_bytes=48 * 2**20),
+        compiler_params=pltpu.CompilerParams(vmem_limit_bytes=32 * 2**20),
         name="place",
     )(
         targets,

time: 41.9 us -> 35.6 us (0.85)
  local copies, waits for them, and re-layouts: 5.08 us -> 0.01 us
  Pallas kernels: 35.8 us -> 34.8 us
    unnamed x14 -> x2, local copies, waits for them, and re-layouts: 5.08 us -> 0.01 us
    pallas_call x1, Pallas kernels: 3.74 us -> 2.73 us  [on_device(): pl.pallas_call(functools.partial(place_kernel, n), out_shape=(shape((rows...]
where the time goes in v3:
time: 35.6 us; the launch traced here: 35.4 us
  Pallas kernels  34.8 us (98%)
  between operations  0.66 us (2%)
    pallas_call x1, Pallas kernels, on_device(): pl.pallas_call(functools.partial(exchange_kernel, n), out_shape=(pltpu.VM...  32 us
    pallas_call x1, Pallas kernels, on_device(): pl.pallas_call(functools.partial(place_kernel, n), out_shape=(shape((rows...  2.73 us

profile of v3, /device:TPU:0, one launch (start us, length us, event | category | flops | bytes accessed | tf_op | source)
XLA Modules:
  0.0 35.4 jit_solution(13304889624843175240)
XLA Ops:
  0.6 0.0 copy-start
  0.6 32.0 %exchange.1 = (bf16[32,128,256]{2,1,0:T(8,128)(2,1)S(1)}, bf16[32,128,256]{2,1,0:T(8,128)(2,1)S(1)}, f32[4,8,2048]{2,1,0:T(8,128)S(1)}, f32[4,8,2048]{2,1,0:T(8,...) custom-call(s32[32]{0:T(128)} %lens_hbm.1, ...), custom_call_target="tpu_custom_call" | custom-call | tf_op jit(solution)/shard_map/exchange/pallas_call | solution.py:335
  32.7 0.0 copy-done
  32.7 2.7 %place.1 = (bf16[32,2048]{1,0:T(8,128)(2,1)}, bf16[32,2048]{1,0:T(8,128)(2,1)}, bf16[32,128,256]{2,1,0:T(8,128)(2,1)}, bf16[32,128,256]{2,1,0:T(8,128)(2,1)}) custom-call(s32[7,1,4]{2,1,0:T(1,128)S(1)} %get-tuple-element.12.targets_hbm, s32[7,1,4]{2,1,0:T(1,128)S(1)} %get-tuple-element.13.landing_hbm, s32[1,4]{1,0:T(1,128)S(1)} %copy-done, ...), custom_call_target="tpu_custom_call" | custom-call | tf_op jit(solution)/shard_map/place/pallas_call | solution.py:385
Async XLA Ops:
  0.6 32.1 %copy-start = (s32[1,4]{1,0:T(1,128)S(1)}, s32[1,4]{1,0:T(1,128)}, u32[]{:S(2)}) copy-start(s32[1,4]{1,0:T(1,128)} %move_rows_hbm.3) | copy-start | bytes 52

commit v4 on v3

--- a/solution.py
+++ b/solution.py
@@ -147,8 +147,9 @@
 
     loads[7].wait()
     qrows = 2 * group
-    offset = lax.broadcasted_iota(jnp.int32, (qrows, ctx), 1) - lax.rem(
-        lax.broadcasted_iota(jnp.int32, (qrows, ctx), 0), 2
+    offset = (
+        lax.broadcasted_iota(jnp.int32, (qrows, ctx), 1)
+        - lax.broadcasted_iota(jnp.int32, (qrows, ctx), 0) // group
     )
     scale = HS ** (-0.5)
 
@@ -168,7 +169,12 @@
             for h in range(heads):
                 at = h * group
                 rows_of = jnp.concatenate(
-                    [query[:, (at + g) * HS : (at + g + 1) * HS] for g in range(group)], axis=0
+                    [
+                        query[t : t + 1, (at + g) * HS : (at + g + 1) * HS]
+                        for t in range(2)
+                        for g in range(group)
+                    ],
+                    axis=0,
                 )
                 s = lax.dot_general(
                     rows_of.astype(jnp.bfloat16),
@@ -182,6 +188,7 @@
         totals = jnp.sum(w, axis=1, keepdims=True)
         w = w.astype(jnp.bfloat16)
         for u in range(UNROLL):
+            seconds = []
             for h in range(heads):
                 at = (u * heads + h) * qrows
                 mixed = lax.dot_general(
@@ -193,10 +200,11 @@
                 mixed = mixed / totals[at : at + qrows]
                 for g in range(group):
                     lanes = pl.ds((h * group + g) * HS, HS)
-                    second = mixed[2 * g + 1 : 2 * g + 2]
-                    first_o[block, low + u : low + u + 1, lanes] = mixed[2 * g : 2 * g + 1]
+                    second = mixed[group + g : group + g + 1]
+                    first_o[block, low + u : low + u + 1, lanes] = mixed[g : g + 1]
                     second_o[block, low + u : low + u + 1, lanes] = second
-                    second_rows[first + u, :, lanes] = second
+                seconds.append(mixed[group:])
+            second_rows[first + u] = jnp.concatenate(seconds, axis=0).astype(jnp.bfloat16)
 
     @pl.loop(0, rows // TILE)
     def _(block):
@@ -298,11 +306,14 @@
         return count + found
 
     lax.fori_loop(0, n - 1, arrive, jnp.int32(0))
-    settled = second[...]
-    slot = lax.broadcasted_iota(jnp.int32, settled.shape, 0)
-    for j in range(moves):
-        settled = jnp.where(slot == dest[j], got_o[origin[j]], settled)
-    second_b[...] = settled.astype(jnp.bfloat16)
+    slot = lax.broadcasted_iota(jnp.int32, (rows, HS), 0)
+    incoming = [got_o[origin[j]].astype(jnp.float32) for j in range(moves)]
+    for i in range(got_o.shape[1]):
+        lanes = slice(i * HS, (i + 1) * HS)
+        part = second[:, lanes]
+        for j in range(moves):
+            part = jnp.where(slot == dest[j], incoming[j][i : i + 1], part)
+        second_b[:, lanes] = part.astype(jnp.bfloat16)
     save_second = pltpu.make_async_copy(second_b, out_second, out_sem.at[3])
     save_second.start()
     save_first.wait()
@@ -340,7 +351,7 @@
             pltpu.VMEM(tiled, f32),
             pltpu.VMEM(tiled, f32),
             pltpu.VMEM((n - 1, 2, ctx, width), bf16),
-            pltpu.VMEM((n - 1, 1, wide), f32),
+            pltpu.VMEM((n - 1, wide // HS, HS), bf16),
             pltpu.VMEM((n - 1, 1, moves), i32),
             pltpu.VMEM((n - 1, 1, moves), i32),
         ),
@@ -355,9 +366,9 @@
             pltpu.VMEM(fresh_keys.shape, bf16),
             pltpu.VMEM((rows, ctx, width), bf16),
             pltpu.VMEM((rows, ctx, width), bf16),
-            pltpu.VMEM((rows, 1, wide), f32),
+            pltpu.VMEM((rows, wide // HS, HS), bf16),
             pltpu.VMEM((n - 1, 2, ctx, width), bf16),
-            pltpu.VMEM((n - 1, 1, wide), f32),
+            pltpu.VMEM((n - 1, wide // HS, HS), bf16),
             pltpu.SemaphoreType.DMA((8,)),
             pltpu.SemaphoreType.DMA((5, n - 1)),
             pltpu.SemaphoreType.DMA((5, n - 1)),

time: 35.6 us -> 35 us (0.983)
  Pallas kernels: 34.8 us -> 34.2 us
    pallas_call x1, Pallas kernels: 32 us -> 31.5 us  [on_device(): pl.pallas_call(functools.partial(exchange_kernel, n), out_shape=(pltpu.VM...]
where the time goes in v4:
time: 35 us; the launch traced here: 34.9 us
  Pallas kernels  34.2 us (98%)
  between operations  0.66 us (2%)
    pallas_call x1, Pallas kernels, on_device(): pl.pallas_call(functools.partial(exchange_kernel, n), out_shape=(pltpu.VM...  31.5 us
    pallas_call x1, Pallas kernels, on_device(): pl.pallas_call(functools.partial(place_kernel, n), out_shape=(shape((rows...  2.73 us

profile of v4, /device:TPU:0, one launch (start us, length us, event | category | flops | bytes accessed | tf_op | source)
XLA Modules:
  0.0 34.9 jit_solution(8166441110341643350)
XLA Ops:
  0.6 0.0 copy-start
  0.6 31.5 %exchange.1 = (bf16[32,128,256]{2,1,0:T(8,128)(2,1)S(1)}, bf16[32,128,256]{2,1,0:T(8,128)(2,1)S(1)}, f32[4,8,2048]{2,1,0:T(8,128)S(1)}, f32[4,8,2048]{2,1,0:T(8,...) custom-call(s32[32]{0:T(128)} %lens_hbm.1, ...), custom_call_target="tpu_custom_call" | custom-call | tf_op jit(solution)/shard_map/exchange/pallas_call | solution.py:346
  32.1 0.0 copy-done
  32.1 2.7 %place.1 = (bf16[32,2048]{1,0:T(8,128)(2,1)}, bf16[32,2048]{1,0:T(8,128)(2,1)}, bf16[32,128,256]{2,1,0:T(8,128)(2,1)}, bf16[32,128,256]{2,1,0:T(8,128)(2,1)}) custom-call(s32[7,1,4]{2,1,0:T(1,128)S(1)} %get-tuple-element.12.targets_hbm, s32[7,1,4]{2,1,0:T(1,128)S(1)} %get-tuple-element.13.landing_hbm, s32[1,4]{1,0:T(1,128)S(1)} %copy-done, ...), custom_call_target="tpu_custom_call" | custom-call | tf_op jit(solution)/shard_map/place/pallas_call | solution.py:396
Async XLA Ops:
  0.6 31.5 %copy-start = (s32[1,4]{1,0:T(1,128)S(1)}, s32[1,4]{1,0:T(1,128)}, u32[]{:S(2)}) copy-start(s32[1,4]{1,0:T(1,128)} %move_rows_hbm.3) | copy-start | bytes 52
